TPU v7x, 256 devices: a whole 4x4x8 slice. The times are simulated.
256 devices in a mesh: dp: 32 (over y, z_hi, x), mp: 8 (over z_lo, core).
Axes of the slice: x: 4, y: 4, z: 8 (z_hi: 2, z_lo: 4; z = z_hi * 4 + z_lo), core: 2. Of those that a mesh axis runs over, the one named last changes fastest.
Arguments:
- tokens: bfloat16 [2048, 6144], P('dp', 'mp'), may hold values from -60 to 60
- norm_gain: float32 [6144], P('mp'), may hold values from 0.5 to 1.5
- w_in: bfloat16 [6144, 24576], P('mp', 'dp'), may hold values from -0.078125 to 0.078125
- b_in: float32 [24576], P('dp'), may hold values from -4 to 4
- w_out: bfloat16 [24576, 6144], P('dp', 'mp'), may hold values from -0.0390625 to 0.0390625
- b_out: float32 [6144], P('mp'), may hold values from -3 to 3
- out_gain: float32 [6144], P('mp'), may hold values from 0.5 to 1.5
- student: bfloat16 [2048, 1024], P(('dp', 'mp')), may hold values from -45 to 45
- w_exit: bfloat16 [1024, 6144], P(None, 'mp'), may hold values from -0.1875 to 0.1875
Outputs:
- mean_loss: float32 [], replicated
- grad_exit: float32 [1024, 6144], P('dp', 'mp')
- grad_student: float32 [2048, 1024], P(('dp', 'mp'))
All inputs are finite; a program needn't handle non-finite values.
Results may differ from a plain program's by a relative error of at most 0.0017.
Values may be sent and summed in bfloat16 or wider, within the bound.
A program may use at most 64 MiB of HBM per device.

v0:
```python
import jax
import jax.numpy as jnp
from jax import lax
from jax.sharding import PartitionSpec as P

epsilon = 1e-06


def shards(tokens, norm_gain, w_in, b_in, w_out, b_out, out_gain, student, w_exit):
    own_rows = tokens.shape[0]
    feature_count = tokens.shape[1] * lax.axis_size("mp")
    total_rows = own_rows * lax.axis_size("dp")
    inputs = tokens.astype(jnp.float32)
    squares = lax.psum(jnp.sum(inputs * inputs, axis=1), "mp")
    scale_in = lax.rsqrt(squares / feature_count + epsilon)
    normed = (inputs * scale_in[:, None] * norm_gain).astype(jnp.bfloat16)
    partial_pre = jnp.dot(
        lax.all_gather(normed, "dp", axis=0, tiled=True), w_in, preferred_element_type=jnp.float32
    )
    preact = lax.psum(partial_pre, "mp") + b_in
    hidden = jax.nn.gelu(preact, approximate=False).astype(jnp.bfloat16)
    rows_now = hidden
    branch = lax.psum_scatter(
        jnp.dot(rows_now, w_out, preferred_element_type=jnp.float32),
        "dp",
        scatter_dimension=0,
        tiled=True,
    )
    features = inputs + branch + b_out
    out_squares = lax.psum(jnp.sum(features * features, axis=1), "mp")
    target = features * lax.rsqrt(out_squares / feature_count + epsilon)[:, None] * out_gain
    learner = lax.all_gather(student, "mp", axis=0, tiled=True)
    predicted = jnp.dot(learner, w_exit, preferred_element_type=jnp.float32)
    errors = predicted - target
    error_sum = lax.psum(jnp.sum(errors * errors), ("dp", "mp"))
    mean_loss = error_sum / (total_rows * feature_count)
    signal = (2.0 * errors).astype(jnp.bfloat16)
    rows_now = signal
    grad_student = lax.psum_scatter(
        lax.dot_general(
            rows_now, w_exit, (((1,), (1,)), ((), ())), preferred_element_type=jnp.float32
        ),
        "mp",
        scatter_dimension=0,
        tiled=True,
    )
    grad_exit = lax.psum_scatter(
        lax.dot_general(
            learner, signal, (((0,), (0,)), ((), ())), preferred_element_type=jnp.float32
        ),
        "dp",
        scatter_dimension=0,
        tiled=True,
    )
    return (mean_loss, grad_exit / total_rows, grad_student)


def solution(mesh):
    placed = (
        P("dp", "mp"),
        P("mp"),
        P("mp", "dp"),
        P("dp"),
        P("dp", "mp"),
        P("mp"),
        P("mp"),
        P(("dp", "mp"), None),
        P(None, "mp"),
    )
    return jax.shard_map(
        shards,
        mesh=mesh,
        in_specs=placed,
        out_specs=(P(), P("dp", "mp"), P(("dp", "mp"), None)),
        check_vma=False,
    )
```

profile of v0, /device:TPU:1, one launch (start us, length us, event | category | flops | bytes accessed | tf_op | source)
XLA Modules:
  0.0 880.7 jit_solution(1066511788309045295)
XLA Ops:
  7.2 0.0 copy-start
  7.2 0.0 all-gather.2.cloned.1.call-start
  7.2 1.1 fusion.12
  8.4 16.2 %psum.28 = f32[64]{0:T(128)S(1)} all-reduce(f32[64]{0:T(128)S(1)} %fusion.12), channel_id=1, replica_groups=mesh['dp'=32,'mp'=8] {'mp'}, use_global_device_ids=true, to_apply=%region_1.0 | all-reduce | flops 64 | bytes 512 | tf_op jit(solution)/shard_map/psum | solution.py:14
  24.5 1.6 fusion.14
  26.2 0.0 all-gather.2.cloned.1.call-update
  26.2 0.0 all-reduce.2.cloned.1.call-start
  26.3 102.3 %all-gather.2.cloned.1.call-done = bf16[2048,768]{1,0:T(8,128)(2,1)} async-done(((bf16[64,768]{1,0:T(8,128)(2,1)}), bf16[2048,768]{1,0:T(8,128)(2,1)}) %all-gather.2.cloned.1.call-update) | async-done | bytes 3145744 | tf_op jit(solution)/shard_map/all_gather | solution.py:18
  128.6 7.5 fusion.49
  136.1 0.0 all-reduce.2.cloned.1.call-update
  136.1 0.0 reduce-scatter.6.cloned.1.call-start
  136.2 142.3 %all-reduce.2.cloned.1.call-done = f32[2048,768]{1,0:T(8,128)} async-done(((f32[2048,768]{1,0:T(8,128)}), f32[2048,768]{1,0:T(8,128)}) %all-reduce.2.cloned.1.call-update) | async-done | bytes 6291472 | tf_op jit(solution)/shard_map/psum | solution.py:20
  278.5 18.8 %fusion.10 = f32[2048,768]{1,0:T(8,128)} fusion(bf16[768,768]{1,0:T(8,128)(2,1)S(1)} %copy-done.5, f32[2048,768]{1,0:T(8,128)} %all-reduce.2.cloned.1.call-done, f32[768]{0:T(1024)S(1)} %copy-done.6), kind=kOutput, calls=%fused_computation.19 | convolution fusion | flops 2519728128 | bytes 13765632 | tf_op jit(solution)/shard_map/dot_general | solution.py:24
  297.3 0.0 reduce-scatter.6.cloned.1.call-update
  297.3 0.0 reduce-scatter.10.cloned.1.call-start
  297.4 0.6 copy-done.3
  298.0 16.4 %all_gather.6 = bf16[64,1024]{1,0:T(8,128)(2,1)S(1)} all-gather(bf16[8,1024]{1,0:T(8,128)(2,1)S(1)} %copy-done.3), channel_id=1, replica_groups=mesh['dp'=32,'mp'=8] {'mp'}, dimensions={0}, use_global_device_ids=true | all-gather | bytes 147456 | tf_op jit(solution)/shard_map/all_gather | solution.py:32
  314.4 252.0 %reduce-scatter.6.cloned.1.call-done = f32[64,768]{1,0:T(8,128)} async-done(((f32[2048,768]{1,0:T(8,128)}), f32[64,768]{1,0:T(8,128)}) %reduce-scatter.6.cloned.1.call-update) | async-done | bytes 196624 | tf_op jit(solution)/shard_map/reduce_scatter | solution.py:23
  566.4 1.1 multiply_reduce_fusion.1
  567.5 15.4 %psum.30 = f32[64]{0:T(128)S(1)} all-reduce(f32[64]{0:T(128)S(1)} %multiply_reduce_fusion.1), channel_id=1, replica_groups=mesh['dp'=32,'mp'=8] {'mp'}, use_global_device_ids=true, to_apply=%region_5.0 | all-reduce | flops 64 | bytes 512 | tf_op jit(solution)/shard_map/psum | solution.py:30
  582.9 1.9 multiply_reduce_fusion
  584.8 2.3 convolution_bitcast_fusion
  587.1 3.5 copy.14
  590.7 0.0 reduce-scatter.10.cloned.1.call-update
  590.7 0.0 reduce-scatter.8.cloned.1.call-start
  590.7 1.3 fusion.16
  592.0 0.0 reduce-scatter.8.cloned.1.call-update
  592.1 74.0 %psum.31 = f32[]{:T(128)} all-reduce(f32[]{:T(128)} %get-tuple-element.9), channel_id=1, replica_groups=mesh['dp'=32,'mp'=8] {'dp','mp'}, use_global_device_ids=true, to_apply=%region_7.0 | all-reduce | flops 1 | bytes 8 | tf_op jit(solution)/shard_map/psum | solution.py:35
  666.7 174.1 %reduce-scatter.10.cloned.1.call-done = f32[32,768]{1,0:T(8,128)} async-done(((f32[1024,768]{1,0:T(8,128)}), f32[32,768]{1,0:T(8,128)}) %reduce-scatter.10.cloned.1.call-update) | async-done | bytes 98320
  840.8 1.1 copy.15
  841.9 0.8 copy.13
  842.7 30.4 %reduce-scatter.8.cloned.1.call-done = f32[8,1024]{1,0:T(8,128)} async-done(((f32[64,1024]{1,0:T(8,128)}), f32[8,1024]{1,0:T(8,128)}) %reduce-scatter.8.cloned.1.call-update) | async-done | bytes 32784 | tf_op jit(solution)/shard_map/reduce_scatter | solution.py:39
  (15 shorter events, 0.1 us)
Async XLA Ops:
  7.2 575.7 %copy-start = (bf16[1024,768]{1,0:T(8,128)(2,1)S(1)}, bf16[1024,768]{1,0:T(8,128)(2,1)}, u32[]{:S(2)}) copy-start(bf16[1024,768]{1,0:T(8,128)(2,1)} %param.17) | copy-start | bytes 4718596
  7.2 121.4 %all-gather.2.cloned.1.call-start = ((), (), s32[]{:S(2)}) async-start(), calls=%async_computation.3 | async-start | bytes 3244032 | tf_op jit(solution)/shard_map/all_gather | solution.py:18
  26.2 252.3 %all-reduce.2.cloned.1.call-start = ((), (), s32[]{:S(2)}) async-start(), calls=%async_computation.4 | async-start | bytes 12582912 | tf_op jit(solution)/shard_map/psum | solution.py:20
  136.1 142.4 %copy-start.5 = (bf16[768,768]{1,0:T(8,128)(2,1)S(1)}, bf16[768,768]{1,0:T(8,128)(2,1)}, u32[]{:S(2)}) copy-start(bf16[768,768]{1,0:T(8,128)(2,1)} %param.13) | copy-start | bytes 3538948
  136.1 142.4 %copy-start.6 = (f32[768]{0:T(1024)S(1)}, f32[768]{0:T(1024)}, u32[]{:S(2)}) copy-start(f32[768]{0:T(1024)} %param.12) | copy-start | bytes 9220
  136.1 430.3 %reduce-scatter.6.cloned.1.call-start = ((), (), s32[]{:S(2)}) async-start(), calls=%async_computation.5 | async-start | bytes 6488064 | tf_op jit(solution)/shard_map/reduce_scatter | solution.py:23
  297.3 0.7 copy-start.3
  297.3 269.1 %copy-start.1 = (bf16[64,768]{1,0:T(8,128)(2,1)S(1)}, bf16[64,768]{1,0:T(8,128)(2,1)}, u32[]{:S(2)}) copy-start(bf16[64,768]{1,0:T(8,128)(2,1)} %param.9) | copy-start | bytes 294916
  297.3 269.1 %copy-start.2 = (f32[768]{0:T(1024)S(1)}, f32[768]{0:T(1024)}, u32[]{:S(2)}) copy-start(f32[768]{0:T(1024)} %param.14) | copy-start | bytes 9220
  297.3 285.6 %copy-start.4 = (f32[768]{0:T(1024)S(1)}, f32[768]{0:T(1024)}, u32[]{:S(2)}) copy-start(f32[768]{0:T(1024)} %param.15) | copy-start | bytes 9220
  297.3 543.5 %reduce-scatter.10.cloned.1.call-start = ((), (), s32[]{:S(2)}) async-start(), calls=%async_computation.7 | async-start | bytes 3244032
  590.7 282.4 %reduce-scatter.8.cloned.1.call-start = ((), (), s32[]{:S(2)}) async-start(), calls=%async_computation.6 | async-start | bytes 294912 | tf_op jit(solution)/shard_map/reduce_scatter | solution.py:39
Sparse Core Ops, SparseCore 0:
  26.3 102.2 all-gather.1
  136.2 142.1 all-reduce.1
  297.4 268.9 reduce-scatter.5
  590.8 249.9 reduce-scatter.9
  843.9 29.1 reduce-scatter.7
where the time goes:
time: 883 us; the launch traced here: 881 us
  waiting for transfers between devices  701 us (79%)
  blocking collectives  122 us (14%)
  matrix products  31.9 us (4%)
  between operations  15.6 us (2%)
    reduce_scatter x1, waiting for transfers between devices, shards(): lax.psum_scatter(jnp.dot(rows_now, w_out, preferred_element_type=jnp.floa...  252 us
    unnamed x6, waiting for transfers between devices  174 us
    psum x1, waiting for transfers between devices, shards(): preact = lax.psum(partial_pre, 'mp') + b_in  142 us
    all_gather x1, waiting for transfers between devices, shards(): lax.all_gather(normed, 'dp', axis=0, tiled=True)  102 us
    psum x1, blocking collectives, shards(): error_sum = lax.psum(jnp.sum(errors * errors), ('dp', 'mp'))  74 us
    reduce_scatter x1, waiting for transfers between devices, shards(): lax.psum_scatter(lax.dot_general(rows_now, w_exit, (((1,), (1,)), ((), ()...  30.4 us
    dot_general x1, matrix products, shards(): jnp.dot(rows_now, w_out, preferred_element_type=jnp.float32)  18.8 us
  transfers between devices with their start and end apart: 5, of which 5 were waited for; matrix products, arithmetic and copies ran while one was open for 0% of the time, Pallas kernels for 0%

commit v1 on v0

v1 whole, which is shorter than its diff:
```python
import math

import jax
import jax.numpy as jnp
from jax import lax
from jax.experimental import pallas as pl
from jax.experimental.pallas import tpu as pltpu
from jax.sharding import PartitionSpec as P

EPS = 1e-06
MESH = pl.DeviceIdType.MESH
F32, BF16 = jnp.float32, jnp.bfloat16

ROWS = 64
HALF = 32
FEAT = 768
HID = 768
STU = 1024
FEATURES = 6144
PATCHES = 2048
TILE = 256
CHUNKS = 8
LAG1, LAG2 = 1, 2


def dot(a, b):
    return jnp.dot(a, b, preferred_element_type=F32)


def kernel(
    tokens, norm_gain, w_in, b_in, w_out, b_out, out_gain, student, w_exit,
    loss_out, exit_out, student_out,
    w_in2, w_out2, w_exit2, vec, vec2, rows32, give, take, sq, xb, part, sent1, got1, hidden, sent2, got2,
    total, sent3, got3, sent4, got4, stu, stut, stua, pred, sig, siga, gstu, gotstu, gexit, gotg, gsum, gotz,
    l1, l2, l3, l4,
    s_core, r_core, s_sq, r_sq, s_x0, r_x0, s_st2, r_st2, s_zh, r_zh, s_rs, r_rs, s_ag, r_ag, s_p2, r_p2, s_p3, r_p3,
    s_stu, r_stu, s_sa, r_sa, s_sig, r_sig, s_gs, r_gs, s_gy, r_gy, s_gz, r_gz, s_l, r_l,
):
    d, m = lax.axis_index("dp"), lax.axis_index("mp")
    x, zh, y = d % 4, (d // 4) % 2, d // 8
    zl, c = m // 2, m % 2

    def at(yy, hh, xx, ll, cc):
        return ((yy * 2 + hh) * 4 + xx, ll * 2 + cc)

    def on_x(i, p=0):
        return at(y, zh, (x + i) % 4, zl, (c + p) % 2)

    def on_y(i):
        return at((y + i) % 4, zh, x, zl, c)

    def run_of(i):
        lo, hi = zl % 2, zl // 2
        lo = (lo + i % 2) % 2
        hi = (hi + i // 2) % 2
        return hi * 2 + lo

    def on_z(i):
        return at(y, zh, x, run_of(i), c)

    far = at(y, 1 - zh, x, zl, c)
    partner = at(y, zh, x, zl, 1 - c)

    def copy(src, dst, ss, rs, to):
        return pltpu.make_async_remote_copy(src, dst, ss, rs, device_id=to, device_id_type=MESH)

    bar = pltpu.get_barrier_semaphore()
    peers = [partner, far]
    for i in range(1, 4):
        peers += [on_x(i), on_x(i, 1), on_y(i), on_z(i)]
    for p in peers:
        pl.semaphore_signal(bar, 1, device_id=p, device_id_type=MESH)
    vec[0:1] = norm_gain[...]
    vec[1:2] = b_out[...]
    vec[2:3] = out_gain[...]
    vec[3:8] = jnp.zeros((5, FEAT), F32)
    rows32[...] = tokens[...].astype(F32).reshape(4, 2, 8, FEAT)
    give[...] = rows32[:, 1 - c].reshape(HALF, FEAT).astype(BF16)
    stu[zl] = student[...].astype(F32)
    pl.semaphore_wait(bar, len(peers))

    core_copies = [
        copy(src, dst, s_core.at[i], r_core.at[i], partner)
        for i, (src, dst) in enumerate(
            [(give, take), (vec, vec2), (w_in, w_in2), (w_out, w_out2), (w_exit, w_exit2)]
        )
    ]
    for cp in core_copies:
        cp.start()
    stu_copies = [copy(stu.at[zl], stu.at[zl], s_stu.at[i - 1], r_stu.at[i - 1], on_z(i)) for i in range(1, 4)]

    core_copies[0].wait_recv()
    own = rows32[:, c].reshape(HALF, FEAT)
    par = take[...].astype(F32)
    sq[0] = jnp.broadcast_to(
        jnp.sum(own * own, axis=1, keepdims=True) + jnp.sum(par * par, axis=1, keepdims=True), (HALF, 128)
    )
    sq_copies = [copy(sq.at[0], sq.at[i], s_sq.at[i - 1], r_sq.at[i - 1], on_z(i)) for i in range(1, 4)]
    for cp in sq_copies:
        cp.start()
    for cp in stu_copies:
        cp.start()
    core_copies[1].wait_recv()
    for cp in sq_copies:
        cp.wait_recv()
    ss = (sq[0] + sq[1]) + (sq[2] + sq[3])
    scale = lax.rsqrt(ss[:, 0:1] / FEATURES + EPS)
    xb[0, 0, 0, 0] = (own * scale * vec[0:1]).astype(BF16)
    xb[0, 0, 1, 0] = (par * scale * vec2[0:1]).astype(BF16)

    x0_copies = [
        copy(xb.at[0, 0, :, 0], xb.at[0, 0, :, 4 - i], s_x0.at[0, i - 1], r_x0.at[0, i - 1], on_x(i)) for i in range(1, 4)
    ]
    y0_copies = [
        copy(xb.at[1, 0, :, 0], xb.at[1, 0, :, 4 - i], s_x0.at[1, i - 1], r_x0.at[1, i - 1], on_y(i)) for i in range(1, 4)
    ]
    zh_copy = copy(xb.at[0, 0, :, 0], xb.at[1, 0, :, 0], s_zh.at[0], r_zh.at[0], far)
    zh_copy.start()
    for cp in x0_copies:
        cp.start()

    def stage2(dz, i):
        to = on_x(i) if dz else on_y(i)
        return copy(xb.at[dz, 0], xb.at[dz, 4 - i], s_st2.at[dz, i - 1], r_st2.at[dz, 4 - i - 1], to)

    zh_copy.wait_recv()
    for cp in y0_copies:
        cp.start()
    for cp in x0_copies:
        cp.wait_recv()
    for i in range(1, 4):
        stage2(0, i).start()
    for cp in y0_copies:
        cp.wait_recv()
    for i in range(1, 4):
        stage2(1, i).start()

    def rs_copy(k, i):
        return copy(sent1.at[k, run_of(i)], got1.at[k, i - 1], s_rs.at[k, i - 1], r_rs.at[k, i - 1], on_z(i))

    def ag_copy(k, i):
        return copy(hidden.at[k, zl], hidden.at[k, zl], s_ag.at[k, i - 1], r_ag.at[k, i - 1], on_z(i))

    def ag_wait(k, i):
        q = run_of(i)
        return copy(hidden.at[k, q], hidden.at[k, q], s_ag.at[k, i - 1], r_ag.at[k, i - 1], on_z(i))

    def p2_copy(dz, e, to):
        k = e * 2 + dz
        return copy(sent2.at[k - 2], got2.at[dz, e - 1], s_p2.at[dz, e - 1], r_p2.at[dz, e - 1], to)

    def p2_target(dz, e):
        return at((y + e * (1 - dz)) % 4, zh, (x + e * dz) % 4, zl, c)

    def first(k):
        dz, e = k % 2, k // 2

        @pl.when(e > 0)
        def _():
            copy(xb.at[dz, 0], xb.at[dz, e], s_st2.at[dz, e - 1], r_st2.at[dz, e - 1], partner).wait_recv()

        for t in range(HID // TILE):
            cols = slice(t * TILE, (t + 1) * TILE)
            a = dot(xb[dz, e, 0].reshape(4 * HALF, FEAT), w_in[:, cols])
            a += dot(xb[dz, e, 1].reshape(4 * HALF, FEAT), w_in2[:, cols])
            a = a.reshape(4, HALF, TILE)
            part[k, :, :, cols] = a
            sent1[k, :, :, cols] = a.astype(BF16)
        for i in range(1, 4):
            rs_copy(k, i).start()

    def middle(k):
        for i in range(1, 4):
            rs_copy(k, i).wait_recv()
        pre = part[k, zl] + b_in[...]
        pre += (got1[k, 0].astype(F32) + got1[k, 1].astype(F32)) + got1[k, 2].astype(F32)
        hidden[k, zl] = (0.5 * pre * (1.0 + lax.erf(pre * math.sqrt(0.5)))).astype(BF16)
        for i in range(1, 4):
            ag_copy(k, i).start()

    def second(k):
        dz, e = k % 2, k // 2
        for i in range(1, 4):
            ag_wait(k, i).wait_recv()
        h = hidden[k].reshape(4 * HALF, HID)
        for f, w in enumerate((w_out, w_out2)):
            for t in range(FEAT // TILE):
                cols = slice(t * TILE, (t + 1) * TILE)
                a = dot(h, w[:, cols]).reshape(4, HALF, TILE)

                @pl.when(e == 0)
                def _():
                    total[dz, f, :, :, cols] = a

                @pl.when(e > 0)
                def _():
                    sent2[k - 2, f, :, :, cols] = a.astype(BF16)

        @pl.when(e > 0)
        def _():
            p2_copy(dz, e, p2_target(dz, e)).start()

    core_copies[2].wait_recv()
    core_copies[3].wait_recv()

    def tick(t, carry):
        @pl.when(t < CHUNKS)
        def _():
            first(t)

        @pl.when((t >= LAG1) & (t < CHUNKS + LAG1))
        def _():
            middle(t - LAG1)

        @pl.when(t >= LAG2)
        def _():
            second(t - LAG2)

        return carry

    lax.fori_loop(0, CHUNKS + LAG2, tick, 0)

    for i in range(1, 4):
        q = run_of(i)
        copy(stu.at[q], stu.at[q], s_stu.at[i - 1], r_stu.at[i - 1], on_z(i)).wait_recv()
    learner = stu[...].reshape(HALF, STU).astype(BF16)
    stua[0, 0] = learner
    combos = [(i, p) for p in range(2) for i in range(4) if i or p]
    sa_copies = [
        copy(stua.at[0, 0], stua.at[(4 - i) % 4, p], s_sa.at[n], r_sa.at[n], on_x(i, p)) for n, (i, p) in enumerate(combos)
    ]
    for cp in sa_copies:
        cp.start()
    core_copies[4].wait_recv()
    for f, w in enumerate((w_exit, w_exit2)):
        for t in range(FEAT // TILE):
            cols = slice(t * TILE, (t + 1) * TILE)
            pred[f, :, cols] = dot(learner, w[:, cols])

    s2 = [None, None]
    p3 = [[None] * 3, [None] * 3]
    for dz in (1, 0):
        for i in range(3):
            p2_copy(dz, i + 1, partner).wait_recv()
        for s in range(3, -1, -1):
            a = total[dz, :, s] + got2[dz, 0, :, s].astype(F32)
            a += got2[dz, 1, :, s].astype(F32) + got2[dz, 2, :, s].astype(F32)
            if s == 0:
                total[dz, :, 0] = a
            else:
                sent3[dz, s - 1] = a.astype(BF16)
                p3[dz][s - 1] = copy(
                    sent3.at[dz, s - 1], got3.at[dz, s - 1], s_p3.at[dz, s - 1], r_p3.at[dz, s - 1],
                    on_y(s) if dz else on_x(s),
                )
                p3[dz][s - 1].start()
    for dz in (1, 0):
        for cp in p3[dz]:
            cp.wait_recv()
        a = total[dz, :, 0] + got3[dz, 0].astype(F32)
        a += got3[dz, 1].astype(F32) + got3[dz, 2].astype(F32)
        if dz:
            sent4[...] = a.astype(BF16)
            back = copy(sent4, got4, s_zh.at[1], r_zh.at[1], far)
            back.start()
        else:
            total[0, :, 0] = a

    for n, (i, p) in enumerate(combos):
        sa_copies[n].wait_recv()
    stut[...] = jnp.transpose(stua[...].reshape(8 * HALF, STU).astype(F32)).astype(BF16).reshape(8, 4, 32, 8 * HALF)

    back.wait_recv()
    sq2 = jnp.zeros((HALF, 1), F32)
    for f in range(2):
        v = vec if f == 0 else vec2
        inputs = rows32[:, c].reshape(HALF, FEAT) if f == 0 else take[...].astype(F32)
        a = inputs + (total[0, f, 0] + got4[f].astype(F32)) + v[1:2]
        total[1, f, 0] = a
        sq2 += jnp.sum(a * a, axis=1, keepdims=True)
    sq[4] = jnp.broadcast_to(sq2, (HALF, 128))
    sq2_copies = [copy(sq.at[4], sq.at[4 + i], s_sq.at[2 + i], r_sq.at[2 + i], on_z(i)) for i in range(1, 4)]
    for cp in sq2_copies:
        cp.start()
    for cp in sq2_copies:
        cp.wait_recv()
    ss = (sq[4] + sq[5]) + (sq[6] + sq[7])
    scale = lax.rsqrt(ss[:, 0:1] / FEATURES + EPS)
    loss = jnp.zeros((8, 128), F32)
    for f in (1, 0):
        v = vec if f == 0 else vec2
        err = pred[f] - total[1, f, 0] * scale * v[2:3]
        sig[f] = (2.0 * err).astype(BF16)
        es = jnp.sum((err * err).reshape(4, 8, FEAT), axis=0)
        for t in range(FEAT // 128):
            loss += es[:, t * 128 : (t + 1) * 128]
    siga[0, 0] = sig[0]

    sig_copies = [
        copy(sig.at[p], siga.at[(4 - i) % 4, p], s_sig.at[n], r_sig.at[n], on_x(i, p)) for n, (i, p) in enumerate(combos)
    ]
    for cp in sig_copies:
        cp.start()
    l1[zl] = loss
    l1_copies = [copy(l1.at[zl], l1.at[zl], s_l.at[i - 1], r_l.at[i - 1], on_z(i)) for i in range(1, 4)]
    for cp in l1_copies:
        cp.start()

    g = lax.dot_general(sig[0], w_exit[...], (((1,), (1,)), ((), ())), preferred_element_type=F32)
    g += lax.dot_general(sig[1], w_exit2[...], (((1,), (1,)), ((), ())), preferred_element_type=F32)
    gstu[...] = g.reshape(4, 8, STU)
    gs_copies = [
        copy(gstu.at[run_of(i)], gotstu.at[i - 1], s_gs.at[i - 1], r_gs.at[i - 1], on_z(i)) for i in range(1, 4)
    ]
    for cp in gs_copies:
        cp.start()

    for cp in sig_copies:
        cp.wait_recv()
    gexit[...] = dot(stut[:, x].reshape(8 * 32, 8 * HALF), siga[...].reshape(8 * HALF, FEAT)).reshape(4, 2, 32, FEAT)
    gy_copies = [
        copy(gexit.at[(y + i) % 4], gotg.at[i - 1], s_gy.at[i - 1], r_gy.at[i - 1], on_y(i)) for i in range(1, 4)
    ]
    for cp in gy_copies:
        cp.start()

    for i in range(1, 4):
        q = run_of(i)
        copy(l1.at[q], l1.at[q], s_l.at[i - 1], r_l.at[i - 1], on_z(i)).wait_recv()
    l2[x, c] = (l1[0] + l1[1]) + (l1[2] + l1[3])
    l2_copies = [copy(l2.at[x, c], l2.at[x, c], s_l.at[3 + n], r_l.at[3 + n], on_x(i, p)) for n, (i, p) in enumerate(combos)]
    for cp in l2_copies:
        cp.start()
    for cp in gs_copies:
        cp.wait_recv()
    student_out[...] = (gstu[zl] + gotstu[0]) + (gotstu[1] + gotstu[2])
    for n, (i, p) in enumerate(combos):
        xx, cc = (x + 4 - i) % 4, (c + p) % 2
        copy(l2.at[xx, cc], l2.at[xx, cc], s_l.at[3 + n], r_l.at[3 + n], partner).wait_recv()
    l3[y] = jnp.sum(l2[...].reshape(8, 8, 128), axis=0)
    l3_copies = [copy(l3.at[y], l3.at[y], s_l.at[9 + i], r_l.at[9 + i], on_y(i)) for i in range(1, 4)]
    for cp in l3_copies:
        cp.start()
    for cp in gy_copies:
        cp.wait_recv()
    gsum[...] = (gexit[y] + gotg[0]) + (gotg[1] + gotg[2])
    gz_copy = copy(gsum.at[1 - zh], gotz, s_gz.at[0], r_gz.at[0], far)
    gz_copy.start()
    for i in range(1, 4):
        yy = (y + 4 - i) % 4
        copy(l3.at[yy], l3.at[yy], s_l.at[9 + i], r_l.at[9 + i], partner).wait_recv()
    l4[zh] = (l3[0] + l3[1]) + (l3[2] + l3[3])
    l4_copy = copy(l4.at[zh], l4.at[zh], s_l.at[13], r_l.at[13], far)
    l4_copy.start()

    for cp in core_copies + stu_copies + sq_copies + x0_copies + y0_copies + [zh_copy, back]:
        cp.wait_send()
    for cp in sa_copies + p3[0] + p3[1] + sq2_copies + sig_copies + l1_copies + gs_copies + gy_copies + l2_copies + l3_copies:
        cp.wait_send()
    for dz in range(2):
        for i in range(1, 4):
            stage2(dz, i).wait_send()
            p2_copy(dz, i, partner).wait_send()

    def drain(k, carry):
        for i in range(1, 4):
            rs_copy(k, i).wait_send()
            ag_copy(k, i).wait_send()
        return carry

    lax.fori_loop(0, CHUNKS, drain, 0)

    copy(l4.at[1 - zh], l4.at[1 - zh], s_l.at[13], r_l.at[13], far).wait_recv()
    loss_out[0, 0] = jnp.sum(l4[0] + l4[1]) / (PATCHES * FEATURES)
    gz_copy.wait_recv()
    exit_out[...] = (gsum[zh] + gotz[...]) / PATCHES
    gz_copy.wait_send()
    l4_copy.wait_send()


def shards(tokens, norm_gain, w_in, b_in, w_out, b_out, out_gain, student, w_exit):
    vm = pltpu.VMEM
    dma = lambda *n: pltpu.SemaphoreType.DMA(n)
    in_vmem = pl.BlockSpec(memory_space=pltpu.VMEM)
    sems = []
    for shape in [(5,), (6,), (2, 3), (2, 3), (2,), (CHUNKS, 3), (CHUNKS, 3), (2, 3), (2, 3), (3,), (7,), (7,), (3,), (3,), (1,), (14,)]:
        sems += [dma(*shape), dma(*shape)]
    loss, g_exit, g_student = pl.pallas_call(
        kernel,
        out_shape=(
            jax.ShapeDtypeStruct((1, 1), F32),
            jax.ShapeDtypeStruct((32, FEAT), F32),
            jax.ShapeDtypeStruct((8, STU), F32),
        ),
        in_specs=[in_vmem] * 9,
        out_specs=(pl.BlockSpec(memory_space=pltpu.SMEM), in_vmem, in_vmem),
        scratch_shapes=[
            vm((FEAT, HID), BF16),
            vm((HID, FEAT), BF16),
            vm((STU, FEAT), BF16),
            vm((8, FEAT), F32),
            vm((8, FEAT), F32),
            vm((4, 2, 8, FEAT), F32),
            vm((HALF, FEAT), BF16),
            vm((HALF, FEAT), BF16),
            vm((8, HALF, 128), F32),
            vm((2, 4, 2, 4, HALF, FEAT), BF16),
            vm((CHUNKS, 4, HALF, HID), F32),
            vm((CHUNKS, 4, HALF, HID), BF16),
            vm((CHUNKS, 3, HALF, HID), BF16),
            vm((CHUNKS, 4, HALF, HID), BF16),
            vm((6, 2, 4, HALF, FEAT), BF16),
            vm((2, 3, 2, 4, HALF, FEAT), BF16),
            vm((2, 2, 4, HALF, FEAT), F32),
            vm((2, 3, 2, HALF, FEAT), BF16),
            vm((2, 3, 2, HALF, FEAT), BF16),
            vm((2, HALF, FEAT), BF16),
            vm((2, HALF, FEAT), BF16),
            vm((4, 8, STU), F32),
            vm((8, 4, 32, 8 * HALF), BF16),
            vm((4, 2, HALF, STU), BF16),
            vm((2, HALF, FEAT), F32),
            vm((2, HALF, FEAT), BF16),
            vm((4, 2, HALF, FEAT), BF16),
            vm((4, 8, STU), F32),
            vm((3, 8, STU), F32),
            vm((4, 2, 32, FEAT), F32),
            vm((3, 2, 32, FEAT), F32),
            vm((2, 32, FEAT), F32),
            vm((32, FEAT), F32),
            vm((4, 8, 128), F32),
            vm((4, 2, 8, 128), F32),
            vm((4, 8, 128), F32),
            vm((2, 8, 128), F32),
        ]
        + sems,
        compiler_params=pltpu.CompilerParams(
            collective_id=0, has_side_effects=True, vmem_limit_bytes=56 * 1024 * 1024
        ),
        name="branch_and_exit",
    )(
        tokens, norm_gain.reshape(1, FEAT), w_in, b_in.reshape(1, HID), w_out, b_out.reshape(1, FEAT),
        out_gain.reshape(1, FEAT), student, w_exit,
    )
    return loss.reshape(()), g_exit, g_student


def solution(mesh):
    placed = (
        P("dp", "mp"),
        P("mp"),
        P("mp", "dp"),
        P("dp"),
        P("dp", "mp"),
        P("mp"),
        P("mp"),
        P(("dp", "mp"), None),
        P(None, "mp"),
    )
    return jax.shard_map(
        shards,
        mesh=mesh,
        in_specs=placed,
        out_specs=(P(), P("dp", "mp"), P(("dp", "mp"), None)),
        check_vma=False,
    )
```

time: 883 us -> 170 us (0.19)
  waiting for transfers between devices: 701 us -> 0 us
  Pallas kernels: 0 us -> 158 us
  blocking collectives: 122 us -> 0 us
  matrix products: 31.9 us -> 0 us
  between operations: 15.6 us -> 2.4 us
    reduce_scatter x2 -> x0, waiting for transfers between devices: 282 us -> none  [the longest x1 252 us: shards(): lax.psum_scatter(jnp.dot(rows_now, w_out, preferred_element_type=jnp.floa...]
    unnamed x6 -> x0, waiting for transfers between devices: 174 us -> none
    pallas_call x0 -> x1, Pallas kernels: none -> 158 us  [shards(): pl.pallas_call(kernel, out_shape=(jax.ShapeDtypeStruct((1, 1), F32), jax....]
    psum x1 -> x0, waiting for transfers between devices: 142 us -> none  [shards(): preact = lax.psum(partial_pre, 'mp') + b_in]
    psum x3 -> x0, blocking collectives: 106 us -> none  [the longest x1 74 us: shards(): error_sum = lax.psum(jnp.sum(errors * errors), ('dp', 'mp'))]
    all_gather x1 -> x0, waiting for transfers between devices: 102 us -> none  [shards(): lax.all_gather(normed, 'dp', axis=0, tiled=True)]
    dot_general x5 -> x0, matrix products: 31.9 us -> none  [the longest x1 18.8 us: shards(): jnp.dot(rows_now, w_out, preferred_element_type=jnp.float32)]
    all_gather x1 -> x0, blocking collectives: 16.4 us -> none  [shards(): learner = lax.all_gather(student, 'mp', axis=0, tiled=True)]
  transfers between devices with their start and end apart: 5 -> 0, of which waited for: 5 -> 0; matrix products, arithmetic and copies ran while one was open for 0% -> 0% of each run, Pallas kernels for 0% -> 0%
where the time goes in v1:
time: 170 us; the launch traced here: 169 us
  Pallas kernels  158 us (93%)
  local copies, waits for them, and re-layouts  7.98 us (5%)
  between operations  2.4 us (1%)
    pallas_call x1, Pallas kernels, shards(): pl.pallas_call(kernel, out_shape=(jax.ShapeDtypeStruct((1, 1), F32), jax....  158 us

profile of v1, /device:TPU:1, one launch (start us, length us, event | category | flops | bytes accessed | tf_op | source)
XLA Modules:
  0.0 168.8 jit_solution(9434673662577601103)
XLA Ops:
  0.6 1.3 reshape.21.norm_gain
  1.9 1.3 reshape.22.b_in
  3.2 1.3 reshape.23.b_out
  4.4 1.2 reshape.24.out_gain
  5.7 158.4 %branch_and_exit.1 = (f32[1,1]{1,0:T(1,128)}, f32[32,768]{1,0:T(8,128)}, f32[8,1024]{1,0:T(8,128)}) custom-call(bf16[64,768]{1,0:T(8,128)(2,1)} %tokens.1, f32[1,768]{1,0:T(1,128)} %reshape.21.norm_gain, bf16[768,768]{1,0:T(8,128)(2,1)} %w_in.1, f32[1,768]{1,0:T(1,128)} %reshape.22.b_in, bf16[768,768]{1,0:T(8,128)(2,1)} %w_out.1, f32[1,768]{1,0:T(1,128)} %reshape.23.b_out, ...), custom_call_target="tpu_custom_call" | custom-call | tf_op jit(solution)/shard_map/branch_and_exit/pallas_call | solution.py:388
  164.8 1.5 copy.16
  166.3 1.4 copy.17

commit v2 on v1

v2 whole, which is shorter than its diff:
```python
import math

import jax
import jax.numpy as jnp
from jax import lax
from jax.experimental import pallas as pl
from jax.experimental.pallas import tpu as pltpu
from jax.sharding import PartitionSpec as P

EPS = 1e-06
MESH = pl.DeviceIdType.MESH
F32, BF16 = jnp.float32, jnp.bfloat16

ROWS = 64
HALF = 32
FEAT = 768
HID = 768
STU = 1024
FEATURES = 6144
PATCHES = 2048
SIDE = FEAT // 2
TILE = 256
CHUNKS = 8
LAG1, LAGF, LAG2 = 1, 2, 3
ORDER = ((0, 0), (1, 0), (0, 1), (1, 1), (1, 3), (1, 2), (0, 3), (0, 2))


def pick(n, table):
    v = table[0]
    for i in range(1, len(table)):
        v = jnp.where(n >= i, table[i], v)
    return v


def dot(a, b):
    return jnp.dot(a, b, preferred_element_type=F32)


def kernel(
    tokens, norm_gain, w_in, b_in, w_out, b_out, out_gain, student, w_exit,
    loss_out, exit_out, student_out,
    w_in2, w_out2, w_exit2, vec, vec2, rows32, give, mine, take, away, sq, xb, part, sent1, got1, hidden, sent2, got2,
    total, sent3, got3, sent4, got4, stu, stq, stut, stut1, stua, stub, pred, sig, sigs, siga, gstu, gotstu, gexit, gotg, gsum, gotz,
    l1, l2, l3, l4,
    s_core, r_core, s_sq, r_sq, s_x0, r_x0, s_st2, r_st2, s_zh, r_zh, s_rs, r_rs, s_ag, r_ag, s_p2, r_p2, s_p3, r_p3,
    s_stu, r_stu, s_sa, r_sa, s_sig, r_sig, s_gs, r_gs, s_gy, r_gy, s_gz, r_gz, s_l, r_l,
):
    d, m = lax.axis_index("dp"), lax.axis_index("mp")
    x, zh, y = d % 4, (d // 4) % 2, d // 8
    zl, c = m // 2, m % 2

    def at(yy, hh, xx, ll, cc):
        return ((yy * 2 + hh) * 4 + xx, ll * 2 + cc)

    def on_x(i, p=0):
        return at(y, zh, (x + i) % 4, zl, (c + p) % 2)

    def on_y(i, p=0):
        return at((y + i) % 4, zh, x, zl, (c + p) % 2)

    def on_ring(a, i, p=0):
        return on_y(i, p) if a else on_x(i, p)

    def run_of(i):
        lo, hi = zl % 2, zl // 2
        lo = (lo + i % 2) % 2
        hi = (hi + i // 2) % 2
        return hi * 2 + lo

    def on_z(i):
        return at(y, zh, x, run_of(i), c)

    far = at(y, 1 - zh, x, zl, c)
    partner = at(y, zh, x, zl, 1 - c)
    far_partner = at(y, 1 - zh, x, zl, 1 - c)

    def copy(src, dst, ss, rs, to):
        return pltpu.make_async_remote_copy(src, dst, ss, rs, device_id=to, device_id_type=MESH)

    bar = pltpu.get_barrier_semaphore()
    peers = [partner, far, far_partner]
    for i in range(1, 4):
        peers += [on_x(i), on_x(i, 1), on_y(i), on_y(i, 1), on_z(i)]
    for p in peers:
        pl.semaphore_signal(bar, 1, device_id=p, device_id_type=MESH)
    vec[0:1] = norm_gain[...].reshape(1, FEAT)
    vec[1:2] = b_out[...].reshape(1, FEAT)
    vec[2:3] = out_gain[...].reshape(1, FEAT)
    vec[3:8] = jnp.zeros((5, FEAT), F32)
    rows32[...] = tokens[...].astype(F32).reshape(4, 2, 8, FEAT)
    give[...] = rows32[:, 1 - c].reshape(HALF, FEAT).astype(BF16)
    mine[...] = rows32[:, c].reshape(HALF, FEAT).astype(BF16)
    stu[zl] = student[...].astype(F32)
    pl.semaphore_wait(bar, len(peers))

    core_copies = [
        copy(src, dst, s_core.at[i], r_core.at[i], partner)
        for i, (src, dst) in enumerate(
            [(give, take), (vec, vec2), (w_in, w_in2), (w_out, w_out2), (w_exit, w_exit2)]
        )
    ]
    far_copies = [
        copy(mine, away.at[0], s_zh.at[0], r_zh.at[0], far),
        copy(give, away.at[1], s_zh.at[1], r_zh.at[1], far_partner),
    ]
    for cp in core_copies[:2] + far_copies + core_copies[2:]:
        cp.start()
    stu_copies = [copy(stu.at[zl], stu.at[zl], s_stu.at[i - 1], r_stu.at[i - 1], on_z(i)) for i in range(1, 4)]

    def squares(n, u, v):
        sq[4 * n] = jnp.broadcast_to(
            jnp.sum(u * u, axis=1, keepdims=True) + jnp.sum(v * v, axis=1, keepdims=True), (HALF, 128)
        )
        cps = [copy(sq.at[4 * n], sq.at[4 * n + i], s_sq.at[n, i - 1], r_sq.at[n, i - 1], on_z(i)) for i in range(1, 4)]
        for cp in cps:
            cp.start()
        return cps

    def scale_of(n, cps):
        for cp in cps:
            cp.wait_recv()
        ss = (sq[4 * n] + sq[4 * n + 1]) + (sq[4 * n + 2] + sq[4 * n + 3])
        return lax.rsqrt(ss[:, 0:1] / FEATURES + EPS)

    core_copies[0].wait_recv()
    own = rows32[:, c].reshape(HALF, FEAT)
    par = take[...].astype(F32)
    sq_copies = squares(0, own, par)
    core_copies[1].wait_recv()
    scale = scale_of(0, sq_copies)
    xb[0, 0, 0, 0] = (own * scale * vec[0:1]).astype(BF16)
    xb[0, 0, 1, 0] = (par * scale * vec2[0:1]).astype(BF16)

    x0_copies = [
        copy(xb.at[0, 0, :, 0], xb.at[0, 0, :, 4 - i], s_x0.at[0, i - 1], r_x0.at[0, i - 1], on_x(i)) for i in range(1, 4)
    ]
    y0_copies = [
        copy(xb.at[1, 0, :, 0], xb.at[1, 0, :, 4 - i], s_x0.at[1, i - 1], r_x0.at[1, i - 1], on_y(i)) for i in range(1, 4)
    ]
    for cp in x0_copies:
        cp.start()
    for cp in far_copies:
        cp.wait_recv()
    own = away[0].astype(F32)
    par = away[1].astype(F32)
    sq1_copies = squares(1, own, par)
    scale = scale_of(1, sq1_copies)
    xb[1, 0, 0, 0] = (own * scale * vec[0:1]).astype(BF16)
    xb[1, 0, 1, 0] = (par * scale * vec2[0:1]).astype(BF16)
    for cp in y0_copies:
        cp.start()
    for cp in stu_copies:
        cp.start()

    def stage2(dz, i):
        to = on_x(i) if dz else on_y(i)
        return copy(xb.at[dz, 0], xb.at[dz, 4 - i], s_st2.at[dz, i - 1], r_st2.at[dz, 4 - i - 1], to)

    for cp in x0_copies:
        cp.wait_recv()
    for i in (1, 3):
        stage2(0, i).start()

    def rs_copy(k, i):
        return copy(sent1.at[k, run_of(i)], got1.at[k, i - 1], s_rs.at[k, i - 1], r_rs.at[k, i - 1], on_z(i))

    def ag_copy(k, i):
        q = run_of(2) if i == 3 else zl
        return copy(hidden.at[k, q], hidden.at[k, q], s_ag.at[k, i - 1], r_ag.at[k, i - 1], on_z(1 if i == 3 else i))

    def ag_wait(k, i):
        q = run_of(i)
        return copy(hidden.at[k, q], hidden.at[k, q], s_ag.at[k, i - 1], r_ag.at[k, i - 1], on_z(i))

    def p2_copy(dz, e, to):
        return copy(sent2.at[dz, e - 1], got2.at[dz, e - 1], s_p2.at[dz, e - 1], r_p2.at[dz, e - 1], to)

    def p2_target(dz, e):
        return at((y + e * (1 - dz)) % 4, zh, (x + e * dz) % 4, zl, c)

    def first(k):
        dz, e = pick(k, [n[0] for n in ORDER]), pick(k, [n[1] for n in ORDER])

        @pl.when(k == 1)
        def _():
            for cp in y0_copies:
                cp.wait_recv()
            for i in (1, 3):
                stage2(1, i).start()
            for dz in range(2):
                stage2(dz, 2).start()

        @pl.when(e > 0)
        def _():
            copy(xb.at[dz, 0], xb.at[dz, e], s_st2.at[dz, e - 1], r_st2.at[dz, e - 1], partner).wait_recv()

        for t in range(HID // TILE):
            cols = slice(t * TILE, (t + 1) * TILE)
            a = dot(xb[dz, e, 0].reshape(4 * HALF, FEAT), w_in[:, cols])
            a += dot(xb[dz, e, 1].reshape(4 * HALF, FEAT), w_in2[:, cols])
            a = a.reshape(4, HALF, TILE)
            part[k, :, :, cols] = a
            sent1[k, :, :, cols] = a.astype(BF16)
        for i in range(1, 4):
            rs_copy(k, i).start()

    def middle(k):
        for i in range(1, 4):
            rs_copy(k, i).wait_recv()
        pre = part[k, zl] + b_in[...].reshape(1, HID)
        pre += (got1[k, 0].astype(F32) + got1[k, 1].astype(F32)) + got1[k, 2].astype(F32)
        hidden[k, zl] = (0.5 * pre * (1.0 + lax.erf(pre * math.sqrt(0.5)))).astype(BF16)
        for i in (2, 1):
            ag_copy(k, i).start()

    def forward(k):
        ag_wait(k, 2).wait_recv()
        ag_copy(k, 3).start()

    def second(k):
        dz, e = pick(k, [n[0] for n in ORDER]), pick(k, [n[1] for n in ORDER])
        for i in (1, 3):
            ag_wait(k, i).wait_recv()
        h = hidden[k].reshape(4 * HALF, HID)
        for f, w in enumerate((w_out, w_out2)):
            for t in range(FEAT // TILE):
                cols = slice(t * TILE, (t + 1) * TILE)
                a = dot(h, w[:, cols]).reshape(4, HALF, TILE)

                @pl.when(e == 0)
                def _():
                    total[dz, f, :, :, cols] = a

                @pl.when(e > 0)
                def _():
                    sent2[dz, e - 1, f, :, :, cols] = a.astype(BF16)

        @pl.when(e > 0)
        def _():
            p2_copy(dz, e, p2_target(dz, e)).start()

    combos = [(i, p) for p in range(2) for i in range(4) if i or p]
    sa_copies = [
        copy(stua.at[0, 0], stua.at[(4 - i) % 4, p], s_sa.at[0, n], r_sa.at[0, n], on_x(i, p))
        for n, (i, p) in enumerate(combos)
    ]
    sa_copies += [
        copy(stq.at[(y + i) % 4], stub.at[(4 - i) % 4, p], s_sa.at[1, n], r_sa.at[1, n], on_y(i, p))
        for n, (i, p) in enumerate(combos)
    ]

    def gather_student():
        for i in range(1, 4):
            q = run_of(i)
            copy(stu.at[q], stu.at[q], s_stu.at[i - 1], r_stu.at[i - 1], on_z(i)).wait_recv()
        stua[0, 0] = stu[...].reshape(HALF, STU).astype(BF16)
        for i in range(4):
            stq[i] = stua[0, 0, :, i * 256 : (i + 1) * 256]
        stub[0, 0] = stq[y]
        for cp in sa_copies:
            cp.start()

    def predict():
        core_copies[4].wait_recv()
        for f, w in enumerate((w_exit, w_exit2)):
            for t in range(FEAT // TILE):
                cols = slice(t * TILE, (t + 1) * TILE)
                pred[f, :, cols] = dot(stua[0, 0], w[:, cols])

    def transpose_student():
        for cp in sa_copies:
            cp.wait_recv()
        stut1[...] = jnp.transpose(stub[...].reshape(8 * HALF, 256).astype(F32)).astype(BF16)
        stut[...] = jnp.transpose(stua[...].reshape(8 * HALF, STU).astype(F32)).astype(BF16).reshape(8, 4, 32, 8 * HALF)

    p3 = [
        [
            copy(
                sent3.at[dz, s - 1], got3.at[dz, s - 1], s_p3.at[dz, s - 1], r_p3.at[dz, s - 1],
                on_y(s) if dz else on_x(s),
            )
            for s in range(1, 4)
        ]
        for dz in range(2)
    ]
    back = copy(sent4, got4, s_zh.at[2], r_zh.at[2], far)

    def reduce2(dz):
        for i in range(3):
            p2_copy(dz, i + 1, partner).wait_recv()
        for s in (2, 1, 3, 0):
            a = total[dz, :, s] + got2[dz, 0, :, s].astype(F32)
            a += got2[dz, 1, :, s].astype(F32) + got2[dz, 2, :, s].astype(F32)
            if s == 0:
                total[dz, :, 0] = a
            else:
                sent3[dz, s - 1] = a.astype(BF16)
                p3[dz][s - 1].start()

    def reduce3(dz):
        for cp in p3[dz]:
            cp.wait_recv()
        a = total[dz, :, 0] + got3[dz, 0].astype(F32)
        a += got3[dz, 1].astype(F32) + got3[dz, 2].astype(F32)
        if dz:
            sent4[...] = a.astype(BF16)
            back.start()
        else:
            total[0, :, 0] = a

    core_copies[2].wait_recv()
    core_copies[3].wait_recv()

    def tick(t, carry):
        @pl.when(t < CHUNKS)
        def _():
            first(t)

        @pl.when((t >= LAG1) & (t < CHUNKS + LAG1))
        def _():
            middle(t - LAG1)

        @pl.when((t >= LAGF) & (t < CHUNKS + LAGF))
        def _():
            forward(t - LAGF)

        @pl.when(t >= LAG2)
        def _():
            second(t - LAG2)

        for when, what in ((2, gather_student), (3, predict), (5, transpose_student)):
            pl.when(t == when)(what)

        @pl.when(t == 9)
        def _():
            reduce2(1)

        return carry

    lax.fori_loop(0, CHUNKS + LAG2, tick, 0)
    reduce3(1)
    reduce2(0)
    reduce3(0)
    back.wait_recv()
    sq2 = jnp.zeros((HALF, 1), F32)
    for f in range(2):
        v = vec if f == 0 else vec2
        inputs = rows32[:, c].reshape(HALF, FEAT) if f == 0 else take[...].astype(F32)
        a = inputs + (total[0, f, 0] + got4[f].astype(F32)) + v[1:2]
        total[1, f, 0] = a
        sq2 += jnp.sum(a * a, axis=1, keepdims=True)
    sq[8] = jnp.broadcast_to(sq2, (HALF, 128))
    sq2_copies = [copy(sq.at[8], sq.at[8 + i], s_sq.at[2, i - 1], r_sq.at[2, i - 1], on_z(i)) for i in range(1, 4)]
    for cp in sq2_copies:
        cp.start()
    scale = scale_of(2, sq2_copies)
    loss = jnp.zeros((8, 128), F32)
    for f in (1, 0):
        v = vec if f == 0 else vec2
        err = pred[f] - total[1, f, 0] * scale * v[2:3]
        sig[f] = (2.0 * err).astype(BF16)
        for a in range(2):
            sigs[a, f] = sig[f, :, a * SIDE : (a + 1) * SIDE]
        es = jnp.sum((err * err).reshape(4, 8, FEAT), axis=0)
        for t in range(FEAT // 128):
            loss += es[:, t * 128 : (t + 1) * 128]
    for a in range(2):
        siga[a, 0, 0] = sigs[a, 0]

    sig_copies = [
        copy(sigs.at[a, p], siga.at[a, (4 - i) % 4, p], s_sig.at[a, n], r_sig.at[a, n], on_ring(a, i, p))
        for n, (i, p) in enumerate(combos)
        for a in range(2)
    ]
    for cp in sig_copies:
        cp.start()
    l1[zl] = loss
    l1_copies = [copy(l1.at[zl], l1.at[zl], s_l.at[i - 1], r_l.at[i - 1], on_z(i)) for i in range(1, 4)]
    for cp in l1_copies:
        cp.start()

    g = lax.dot_general(sig[0], w_exit[...], (((1,), (1,)), ((), ())), preferred_element_type=F32)
    g += lax.dot_general(sig[1], w_exit2[...], (((1,), (1,)), ((), ())), preferred_element_type=F32)
    gstu[...] = g.reshape(4, 8, STU)
    gs_copies = [
        copy(gstu.at[run_of(i)], gotstu.at[i - 1], s_gs.at[i - 1], r_gs.at[i - 1], on_z(i)) for i in range(1, 4)
    ]
    for cp in gs_copies:
        cp.start()

    for cp in sig_copies:
        cp.wait_recv()
    gexit[0] = dot(stut[:, x].reshape(256, 8 * HALF), siga[0].reshape(8 * HALF, SIDE)).reshape(4, 2, 32, SIDE)
    g = dot(stut1[...], siga[1].reshape(8 * HALF, SIDE)).reshape(2, 4, 32, SIDE)
    for h in range(2):
        gexit[1, :, h] = g[h]
    gy_copies = [
        copy(
            gexit.at[a, ((x if a else y) + i) % 4], gotg.at[a, i - 1], s_gy.at[a, i - 1], r_gy.at[a, i - 1],
            on_ring(1 - a, i),
        )
        for i in range(1, 4)
        for a in range(2)
    ]
    for cp in gy_copies:
        cp.start()

    for i in range(1, 4):
        q = run_of(i)
        copy(l1.at[q], l1.at[q], s_l.at[i - 1], r_l.at[i - 1], on_z(i)).wait_recv()
    l2[x, c] = (l1[0] + l1[1]) + (l1[2] + l1[3])
    l2_copies = [copy(l2.at[x, c], l2.at[x, c], s_l.at[3 + n], r_l.at[3 + n], on_x(i, p)) for n, (i, p) in enumerate(combos)]
    for cp in l2_copies:
        cp.start()
    for cp in gs_copies:
        cp.wait_recv()
    student_out[...] = (gstu[zl] + gotstu[0]) + (gotstu[1] + gotstu[2])
    for n, (i, p) in enumerate(combos):
        xx, cc = (x + 4 - i) % 4, (c + p) % 2
        copy(l2.at[xx, cc], l2.at[xx, cc], s_l.at[3 + n], r_l.at[3 + n], partner).wait_recv()
    l3[y] = jnp.sum(l2[...].reshape(8, 8, 128), axis=0)
    l3_copies = [copy(l3.at[y], l3.at[y], s_l.at[9 + i], r_l.at[9 + i], on_y(i)) for i in range(1, 4)]
    for cp in l3_copies:
        cp.start()
    for cp in gy_copies:
        cp.wait_recv()
    for a in range(2):
        gsum[:, a] = (gexit[a, x if a else y] + gotg[a, 0]) + (gotg[a, 1] + gotg[a, 2])
    gz_copy = copy(gsum.at[1 - zh], gotz, s_gz.at[0], r_gz.at[0], far)
    gz_copy.start()
    for i in range(1, 4):
        yy = (y + 4 - i) % 4
        copy(l3.at[yy], l3.at[yy], s_l.at[9 + i], r_l.at[9 + i], partner).wait_recv()
    l4[zh] = (l3[0] + l3[1]) + (l3[2] + l3[3])
    l4_copy = copy(l4.at[zh], l4.at[zh], s_l.at[13], r_l.at[13], far)
    l4_copy.start()

    for cp in core_copies + stu_copies + sq_copies + sq1_copies + x0_copies + y0_copies + far_copies + [back]:
        cp.wait_send()
    for cp in sa_copies + p3[0] + p3[1] + sq2_copies + sig_copies + l1_copies + gs_copies + gy_copies + l2_copies + l3_copies:
        cp.wait_send()
    for dz in range(2):
        for i in range(1, 4):
            stage2(dz, i).wait_send()
            p2_copy(dz, i, partner).wait_send()

    def drain(k, carry):
        for i in range(1, 4):
            rs_copy(k, i).wait_send()
            ag_copy(k, i).wait_send()
        return carry

    lax.fori_loop(0, CHUNKS, drain, 0)

    copy(l4.at[1 - zh], l4.at[1 - zh], s_l.at[13], r_l.at[13], far).wait_recv()
    loss_out[0, 0] = jnp.sum(l4[0] + l4[1]) / (PATCHES * FEATURES)
    gz_copy.wait_recv()
    for a in range(2):
        exit_out[:, a * SIDE : (a + 1) * SIDE] = (gsum[zh, a] + gotz[a]) / PATCHES
    gz_copy.wait_send()
    l4_copy.wait_send()


def shards(tokens, norm_gain, w_in, b_in, w_out, b_out, out_gain, student, w_exit):
    vm = pltpu.VMEM
    dma = lambda *n: pltpu.SemaphoreType.DMA(n)
    in_vmem = pl.BlockSpec(memory_space=pltpu.VMEM)
    sems = []
    for shape in [(5,), (3, 3), (2, 3), (2, 3), (3,), (CHUNKS, 3), (CHUNKS, 3), (2, 3), (2, 3), (3,), (2, 7), (2, 7), (3,), (2, 3), (1,), (14,)]:
        sems += [dma(*shape), dma(*shape)]
    loss, g_exit, g_student = pl.pallas_call(
        kernel,
        out_shape=(
            jax.ShapeDtypeStruct((1, 1), F32),
            jax.ShapeDtypeStruct((32, FEAT), F32),
            jax.ShapeDtypeStruct((8, STU), F32),
        ),
        in_specs=[in_vmem] * 9,
        out_specs=(pl.BlockSpec(memory_space=pltpu.SMEM), in_vmem, in_vmem),
        scratch_shapes=[
            vm((FEAT, HID), BF16),
            vm((HID, FEAT), BF16),
            vm((STU, FEAT), BF16),
            vm((8, FEAT), F32),
            vm((8, FEAT), F32),
            vm((4, 2, 8, FEAT), F32),
            vm((HALF, FEAT), BF16),
            vm((HALF, FEAT), BF16),
            vm((HALF, FEAT), BF16),
            vm((2, HALF, FEAT), BF16),
            vm((12, HALF, 128), F32),
            vm((2, 4, 2, 4, HALF, FEAT), BF16),
            vm((CHUNKS, 4, HALF, HID), F32),
            vm((CHUNKS, 4, HALF, HID), BF16),
            vm((CHUNKS, 3, HALF, HID), BF16),
            vm((CHUNKS, 4, HALF, HID), BF16),
            vm((2, 3, 2, 4, HALF, FEAT), BF16),
            vm((2, 3, 2, 4, HALF, FEAT), BF16),
            vm((2, 2, 4, HALF, FEAT), F32),
            vm((2, 3, 2, HALF, FEAT), BF16),
            vm((2, 3, 2, HALF, FEAT), BF16),
            vm((2, HALF, FEAT), BF16),
            vm((2, HALF, FEAT), BF16),
            vm((4, 8, STU), F32),
            vm((4, HALF, 256), BF16),
            vm((8, 4, 32, 8 * HALF), BF16),
            vm((256, 8 * HALF), BF16),
            vm((4, 2, HALF, STU), BF16),
            vm((4, 2, HALF, 256), BF16),
            vm((2, HALF, FEAT), F32),
            vm((2, HALF, FEAT), BF16),
            vm((2, 2, HALF, SIDE), BF16),
            vm((2, 4, 2, HALF, SIDE), BF16),
            vm((4, 8, STU), F32),
            vm((3, 8, STU), F32),
            vm((2, 4, 2, 32, SIDE), F32),
            vm((2, 3, 2, 32, SIDE), F32),
            vm((2, 2, 32, SIDE), F32),
            vm((2, 32, SIDE), F32),
            vm((4, 8, 128), F32),
            vm((4, 2, 8, 128), F32),
            vm((4, 8, 128), F32),
            vm((2, 8, 128), F32),
        ]
        + sems,
        compiler_params=pltpu.CompilerParams(
            collective_id=0, has_side_effects=True, vmem_limit_bytes=56 * 1024 * 1024
        ),
        name="branch_and_exit",
    )(
        tokens, norm_gain, w_in, b_in, w_out, b_out,
        out_gain, student, w_exit,
    )
    return loss.reshape(()), g_exit, g_student


def solution(mesh):
    placed = (
        P("dp", "mp"),
        P("mp"),
        P("mp", "dp"),
        P("dp"),
        P("dp", "mp"),
        P("mp"),
        P("mp"),
        P(("dp", "mp"), None),
        P(None, "mp"),
    )
    return jax.shard_map(
        shards,
        mesh=mesh,
        in_specs=placed,
        out_specs=(P(), P("dp", "mp"), P(("dp", "mp"), None)),
        check_vma=False,
    )
```

time: 170 us -> 147 us (0.86)
  Pallas kernels: 158 us -> 142 us
  local copies, waits for them, and re-layouts: 7.98 us -> 2.91 us
    pallas_call x1, Pallas kernels: 158 us -> 142 us  [shards(): pl.pallas_call(kernel, out_shape=(jax.ShapeDtypeStruct((1, 1), F32), jax....]
    reshape x4 -> x0, local copies, waits for them, and re-layouts: 5.07 us -> none  [the longest x1 1.28 us: shards(): b_out.reshape(1, FEAT)]
where the time goes in v2:
time: 147 us
  Pallas kernels  142 us (97%)
  local copies, waits for them, and re-layouts  2.91 us (2%)
  between operations  2.45 us (2%)
    pallas_call x1, Pallas kernels, shards(): pl.pallas_call(kernel, out_shape=(jax.ShapeDtypeStruct((1, 1), F32), jax....  142 us

profile of v2, /device:TPU:1, one launch (start us, length us, event | category | flops | bytes accessed | tf_op | source)
XLA Modules:
  0.0 146.9 jit_solution(10217493059899656769)
XLA Ops:
  0.6 141.6 %branch_and_exit.1 = (f32[1,1]{1,0:T(1,128)}, f32[32,768]{1,0:T(8,128)}, f32[8,1024]{1,0:T(8,128)}) custom-call(bf16[64,768]{1,0:T(8,128)(2,1)} %tokens.1, f32[768]{0:T(1024)} %norm_gain.1, bf16[768,768]{1,0:T(8,128)(2,1)} %w_in.1, f32[768]{0:T(1024)} %b_in.1, bf16[768,768]{1,0:T(8,128)(2,1)} %w_out.1, f32[768]{0:T(1024)} %b_out.1, f32[768]{0:T(1024)} %out_gain.1, ...), custom_call_target="tpu_custom_call" | custom-call | tf_op jit(solution)/shard_map/branch_and_exit/pallas_call | solution.py:471
  142.9 1.5 %copy.16 = f32[32,768]{1,0:T(8,128)} copy(f32[32,768]{1,0:T(8,128)} %get-tuple-element.13) | data formatting | bytes 196608
  144.4 1.4 copy.17

commit v3 on v2

--- a/solution.py
+++ b/solution.py
@@ -21,7 +21,8 @@
 SIDE = FEAT // 2
 TILE = 256
 CHUNKS = 8
-LAG1, LAGF, LAG2 = 1, 2, 3
+LAG1, LAGF, LAG2, LAG3 = 1, 2, 3, 4
+BACK = 10
 ORDER = ((0, 0), (1, 0), (0, 1), (1, 1), (1, 3), (1, 2), (0, 3), (0, 2))
 
 
@@ -37,12 +38,12 @@
 
 
 def kernel(
-    tokens, norm_gain, w_in, b_in, w_out, b_out, out_gain, student, w_exit,
+    tokens, norm_gain, w_in_hbm, b_in, w_out_hbm, b_out, out_gain, student, w_exit_hbm,
     loss_out, exit_out, student_out,
-    w_in2, w_out2, w_exit2, vec, vec2, rows32, give, mine, take, away, sq, xb, part, sent1, got1, hidden, sent2, got2,
+    w_in, w_out, w_exit, w_in2, w_out2, w_exit2, vec, vec2, rows32, give, mine, take, away, sq, xb, part, sent1, got1, hidden, sent2, got2,
     total, sent3, got3, sent4, got4, stu, stq, stut, stut1, stua, stub, pred, sig, sigs, siga, gstu, gotstu, gexit, gotg, gsum, gotz,
     l1, l2, l3, l4,
-    s_core, r_core, s_sq, r_sq, s_x0, r_x0, s_st2, r_st2, s_zh, r_zh, s_rs, r_rs, s_ag, r_ag, s_p2, r_p2, s_p3, r_p3,
+    s_load, s_core, r_core, s_sq, r_sq, s_x0, r_x0, s_st2, r_st2, s_zh, r_zh, s_rs, r_rs, s_ag, r_ag, s_p2, r_p2, s_p3, r_p3,
     s_stu, r_stu, s_sa, r_sa, s_sig, r_sig, s_gs, r_gs, s_gy, r_gy, s_gz, r_gz, s_l, r_l,
 ):
     d, m = lax.axis_index("dp"), lax.axis_index("mp")
@@ -83,6 +84,12 @@
         peers += [on_x(i), on_x(i, 1), on_y(i), on_y(i, 1), on_z(i)]
     for p in peers:
         pl.semaphore_signal(bar, 1, device_id=p, device_id_type=MESH)
+    loads = [
+        pltpu.make_async_copy(src, dst, s_load.at[i])
+        for i, (src, dst) in enumerate([(w_in_hbm, w_in), (w_out_hbm, w_out), (w_exit_hbm, w_exit)])
+    ]
+    for cp in loads:
+        cp.start()
     vec[0:1] = norm_gain[...].reshape(1, FEAT)
     vec[1:2] = b_out[...].reshape(1, FEAT)
     vec[2:3] = out_gain[...].reshape(1, FEAT)
@@ -103,7 +110,7 @@
         copy(mine, away.at[0], s_zh.at[0], r_zh.at[0], far),
         copy(give, away.at[1], s_zh.at[1], r_zh.at[1], far_partner),
     ]
-    for cp in core_copies[:2] + far_copies + core_copies[2:]:
+    for cp in core_copies[:2] + far_copies:
         cp.start()
     stu_copies = [copy(stu.at[zl], stu.at[zl], s_stu.at[i - 1], r_stu.at[i - 1], on_z(i)) for i in range(1, 4)]
 
@@ -122,6 +129,9 @@
         ss = (sq[4 * n] + sq[4 * n + 1]) + (sq[4 * n + 2] + sq[4 * n + 3])
         return lax.rsqrt(ss[:, 0:1] / FEATURES + EPS)
 
+    for i in range(3):
+        loads[i].wait()
+        core_copies[2 + i].start()
     core_copies[0].wait_recv()
     own = rows32[:, c].reshape(HALF, FEAT)
     par = take[...].astype(F32)
@@ -131,35 +141,36 @@
     xb[0, 0, 0, 0] = (own * scale * vec[0:1]).astype(BF16)
     xb[0, 0, 1, 0] = (par * scale * vec2[0:1]).astype(BF16)
 
-    x0_copies = [
-        copy(xb.at[0, 0, :, 0], xb.at[0, 0, :, 4 - i], s_x0.at[0, i - 1], r_x0.at[0, i - 1], on_x(i)) for i in range(1, 4)
-    ]
-    y0_copies = [
-        copy(xb.at[1, 0, :, 0], xb.at[1, 0, :, 4 - i], s_x0.at[1, i - 1], r_x0.at[1, i - 1], on_y(i)) for i in range(1, 4)
-    ]
-    for cp in x0_copies:
-        cp.start()
-    for cp in far_copies:
-        cp.wait_recv()
-    own = away[0].astype(F32)
-    par = away[1].astype(F32)
-    sq1_copies = squares(1, own, par)
-    scale = scale_of(1, sq1_copies)
-    xb[1, 0, 0, 0] = (own * scale * vec[0:1]).astype(BF16)
-    xb[1, 0, 1, 0] = (par * scale * vec2[0:1]).astype(BF16)
-    for cp in y0_copies:
-        cp.start()
+    def stage1(dz, i):
+        return copy(xb.at[dz, 0, :, 0], xb.at[dz, 4 - i, :, 0], s_x0.at[dz, i - 1], r_x0.at[dz, i - 1], on_ring(dz, i))
+
+    def stage2(dz, s, i):
+        to = at((y + i * (1 - dz)) % 4, zh, (x + i * dz) % 4, zl, c)
+        return copy(xb.at[dz, s, :, 0], xb.at[dz, s, :, 4 - i], s_st2.at[dz, s, i - 1], r_st2.at[dz, s, i - 1], to)
+
+    for dz in range(2):
+        if dz:
+            for cp in far_copies:
+                cp.wait_recv()
+            own = away[0].astype(F32)
+            par = away[1].astype(F32)
+            sq1_copies = squares(1, own, par)
+            scale = scale_of(1, sq1_copies)
+            xb[1, 0, 0, 0] = (own * scale * vec[0:1]).astype(BF16)
+            xb[1, 0, 1, 0] = (par * scale * vec2[0:1]).astype(BF16)
+        for i in (1, 3, 2):
+            stage1(dz, i).start()
+            stage2(dz, 0, i).start()
     for cp in stu_copies:
         cp.start()
 
-    def stage2(dz, i):
-        to = on_x(i) if dz else on_y(i)
-        return copy(xb.at[dz, 0], xb.at[dz, 4 - i], s_st2.at[dz, i - 1], r_st2.at[dz, 4 - i - 1], to)
-
-    for cp in x0_copies:
-        cp.wait_recv()
-    for i in (1, 3):
-        stage2(0, i).start()
+    def pass_on(dz):
+        for s in (1, 3, 2):
+            stage1(dz, 4 - s).wait_recv()
+            for i in (1, 3, 2):
+                stage2(dz, s, i).start()
+
+    pass_on(0)
 
     def rs_copy(k, i):
         return copy(sent1.at[k, run_of(i)], got1.at[k, i - 1], s_rs.at[k, i - 1], r_rs.at[k, i - 1], on_z(i))
@@ -172,27 +183,26 @@
         q = run_of(i)
         return copy(hidden.at[k, q], hidden.at[k, q], s_ag.at[k, i - 1], r_ag.at[k, i - 1], on_z(i))
 
-    def p2_copy(dz, e, to):
-        return copy(sent2.at[dz, e - 1], got2.at[dz, e - 1], s_p2.at[dz, e - 1], r_p2.at[dz, e - 1], to)
-
-    def p2_target(dz, e):
-        return at((y + e * (1 - dz)) % 4, zh, (x + e * dz) % 4, zl, c)
+    def p2_copy(dz, e, r):
+        to = at((y + r * (1 - dz)) % 4, zh, (x + r * dz) % 4, zl, c)
+        return copy(sent2.at[dz, e, r - 1], got2.at[dz, e, r - 1], s_p2.at[dz, e, r - 1], r_p2.at[dz, e, r - 1], to)
+
+    def p3_copy(dz, e):
+        to = at((y + e * dz) % 4, zh, (x + e * (1 - dz)) % 4, zl, c)
+        return copy(sent3.at[dz, e - 1], got3.at[dz, e - 1], s_p3.at[dz, e - 1], r_p3.at[dz, e - 1], to)
+
+    def place_of(k):
+        return pick(k, [n[0] for n in ORDER]), pick(k, [n[1] for n in ORDER])
 
     def first(k):
-        dz, e = pick(k, [n[0] for n in ORDER]), pick(k, [n[1] for n in ORDER])
+        dz, e = place_of(k)
 
         @pl.when(k == 1)
         def _():
-            for cp in y0_copies:
-                cp.wait_recv()
-            for i in (1, 3):
-                stage2(1, i).start()
-            for dz in range(2):
-                stage2(dz, 2).start()
-
-        @pl.when(e > 0)
-        def _():
-            copy(xb.at[dz, 0], xb.at[dz, e], s_st2.at[dz, e - 1], r_st2.at[dz, e - 1], partner).wait_recv()
+            pass_on(1)
+
+        for r in range(1, 4):
+            copy(xb.at[dz, e, :, r], xb.at[dz, e, :, r], s_st2.at[dz, e, 3 - r], r_st2.at[dz, e, 3 - r], partner).wait_recv()
 
         for t in range(HID // TILE):
             cols = slice(t * TILE, (t + 1) * TILE)
@@ -218,7 +228,7 @@
         ag_copy(k, 3).start()
 
     def second(k):
-        dz, e = pick(k, [n[0] for n in ORDER]), pick(k, [n[1] for n in ORDER])
+        dz, e = place_of(k)
         for i in (1, 3):
             ag_wait(k, i).wait_recv()
         h = hidden[k].reshape(4 * HALF, HID)
@@ -226,18 +236,26 @@
             for t in range(FEAT // TILE):
                 cols = slice(t * TILE, (t + 1) * TILE)
                 a = dot(h, w[:, cols]).reshape(4, HALF, TILE)
-
-                @pl.when(e == 0)
-                def _():
-                    total[dz, f, :, :, cols] = a
-
-                @pl.when(e > 0)
-                def _():
-                    sent2[dz, e - 1, f, :, :, cols] = a.astype(BF16)
+                total[dz, e, f, :, cols] = a[0]
+                for r in range(1, 4):
+                    sent2[dz, e, r - 1, f, :, cols] = a[r].astype(BF16)
+        for r in (2, 1, 3):
+            p2_copy(dz, e, r).start()
+
+    def reduce2(k):
+        dz, e = place_of(k)
+        for r in range(1, 4):
+            p2_copy(dz, e, r).wait_recv()
+        a = (total[dz, e] + got2[dz, e, 0].astype(F32)) + (got2[dz, e, 1].astype(F32) + got2[dz, e, 2].astype(F32))
+
+        @pl.when(e == 0)
+        def _():
+            total[dz, 0] = a
 
         @pl.when(e > 0)
         def _():
-            p2_copy(dz, e, p2_target(dz, e)).start()
+            sent3[dz, e - 1] = a.astype(BF16)
+            p3_copy(dz, e).start()
 
     combos = [(i, p) for p in range(2) for i in range(4) if i or p]
     sa_copies = [
@@ -273,40 +291,17 @@
         stut1[...] = jnp.transpose(stub[...].reshape(8 * HALF, 256).astype(F32)).astype(BF16)
         stut[...] = jnp.transpose(stua[...].reshape(8 * HALF, STU).astype(F32)).astype(BF16).reshape(8, 4, 32, 8 * HALF)
 
-    p3 = [
-        [
-            copy(
-                sent3.at[dz, s - 1], got3.at[dz, s - 1], s_p3.at[dz, s - 1], r_p3.at[dz, s - 1],
-                on_y(s) if dz else on_x(s),
-            )
-            for s in range(1, 4)
-        ]
-        for dz in range(2)
-    ]
     back = copy(sent4, got4, s_zh.at[2], r_zh.at[2], far)
 
-    def reduce2(dz):
-        for i in range(3):
-            p2_copy(dz, i + 1, partner).wait_recv()
-        for s in (2, 1, 3, 0):
-            a = total[dz, :, s] + got2[dz, 0, :, s].astype(F32)
-            a += got2[dz, 1, :, s].astype(F32) + got2[dz, 2, :, s].astype(F32)
-            if s == 0:
-                total[dz, :, 0] = a
-            else:
-                sent3[dz, s - 1] = a.astype(BF16)
-                p3[dz][s - 1].start()
-
     def reduce3(dz):
-        for cp in p3[dz]:
-            cp.wait_recv()
-        a = total[dz, :, 0] + got3[dz, 0].astype(F32)
-        a += got3[dz, 1].astype(F32) + got3[dz, 2].astype(F32)
+        for e in range(1, 4):
+            p3_copy(dz, e).wait_recv()
+        a = (total[dz, 0] + got3[dz, 0].astype(F32)) + (got3[dz, 1].astype(F32) + got3[dz, 2].astype(F32))
         if dz:
             sent4[...] = a.astype(BF16)
             back.start()
         else:
-            total[0, :, 0] = a
+            total[0, 0] = a
 
     core_copies[2].wait_recv()
     core_copies[3].wait_recv()
@@ -324,30 +319,32 @@
         def _():
             forward(t - LAGF)
 
-        @pl.when(t >= LAG2)
+        @pl.when((t >= LAG2) & (t < CHUNKS + LAG2))
         def _():
             second(t - LAG2)
+
+        @pl.when(t >= LAG3)
+        def _():
+            reduce2(t - LAG3)
 
         for when, what in ((2, gather_student), (3, predict), (5, transpose_student)):
             pl.when(t == when)(what)
 
-        @pl.when(t == 9)
-        def _():
-            reduce2(1)
+        @pl.when(t == BACK)
+        def _():
+            reduce3(1)
 
         return carry
 
-    lax.fori_loop(0, CHUNKS + LAG2, tick, 0)
-    reduce3(1)
-    reduce2(0)
+    lax.fori_loop(0, CHUNKS + LAG3, tick, 0)
     reduce3(0)
     back.wait_recv()
     sq2 = jnp.zeros((HALF, 1), F32)
     for f in range(2):
         v = vec if f == 0 else vec2
         inputs = rows32[:, c].reshape(HALF, FEAT) if f == 0 else take[...].astype(F32)
-        a = inputs + (total[0, f, 0] + got4[f].astype(F32)) + v[1:2]
-        total[1, f, 0] = a
+        a = inputs + (total[0, 0, f] + got4[f].astype(F32)) + v[1:2]
+        total[1, 0, f] = a
         sq2 += jnp.sum(a * a, axis=1, keepdims=True)
     sq[8] = jnp.broadcast_to(sq2, (HALF, 128))
     sq2_copies = [copy(sq.at[8], sq.at[8 + i], s_sq.at[2, i - 1], r_sq.at[2, i - 1], on_z(i)) for i in range(1, 4)]
@@ -357,7 +354,7 @@
     loss = jnp.zeros((8, 128), F32)
     for f in (1, 0):
         v = vec if f == 0 else vec2
-        err = pred[f] - total[1, f, 0] * scale * v[2:3]
+        err = pred[f] - total[1, 0, f] * scale * v[2:3]
         sig[f] = (2.0 * err).astype(BF16)
         for a in range(2):
             sigs[a, f] = sig[f, :, a * SIDE : (a + 1) * SIDE]
@@ -435,19 +432,21 @@
     l4_copy = copy(l4.at[zh], l4.at[zh], s_l.at[13], r_l.at[13], far)
     l4_copy.start()
 
-    for cp in core_copies + stu_copies + sq_copies + sq1_copies + x0_copies + y0_copies + far_copies + [back]:
+    for cp in core_copies + stu_copies + sq_copies + sq1_copies + far_copies + [back]:
         cp.wait_send()
-    for cp in sa_copies + p3[0] + p3[1] + sq2_copies + sig_copies + l1_copies + gs_copies + gy_copies + l2_copies + l3_copies:
+    for cp in sa_copies + sq2_copies + sig_copies + l1_copies + gs_copies + gy_copies + l2_copies + l3_copies:
         cp.wait_send()
     for dz in range(2):
         for i in range(1, 4):
-            stage2(dz, i).wait_send()
-            p2_copy(dz, i, partner).wait_send()
+            stage1(dz, i).wait_send()
+            p3_copy(dz, i).wait_send()
 
     def drain(k, carry):
         for i in range(1, 4):
             rs_copy(k, i).wait_send()
             ag_copy(k, i).wait_send()
+            stage2(k // 4, k % 4, i).wait_send()
+            p2_copy(k // 4, k % 4, i).wait_send()
         return carry
 
     lax.fori_loop(0, CHUNKS, drain, 0)
@@ -461,12 +460,18 @@
     l4_copy.wait_send()
 
 
+def place(a, b, a_out, b_out):
+    a_out[...] = a[...]
+    b_out[...] = b[...]
+
+
 def shards(tokens, norm_gain, w_in, b_in, w_out, b_out, out_gain, student, w_exit):
     vm = pltpu.VMEM
     dma = lambda *n: pltpu.SemaphoreType.DMA(n)
     in_vmem = pl.BlockSpec(memory_space=pltpu.VMEM)
-    sems = []
-    for shape in [(5,), (3, 3), (2, 3), (2, 3), (3,), (CHUNKS, 3), (CHUNKS, 3), (2, 3), (2, 3), (3,), (2, 7), (2, 7), (3,), (2, 3), (1,), (14,)]:
+    in_hbm = pl.BlockSpec(memory_space=pl.ANY)
+    sems = [dma(3)]
+    for shape in [(5,), (3, 3), (2, 3), (2, 4, 3), (3,), (CHUNKS, 3), (CHUNKS, 3), (2, 4, 3), (2, 3), (3,), (2, 7), (2, 7), (3,), (2, 3), (1,), (14,)]:
         sems += [dma(*shape), dma(*shape)]
     loss, g_exit, g_student = pl.pallas_call(
         kernel,
@@ -475,9 +480,12 @@
             jax.ShapeDtypeStruct((32, FEAT), F32),
             jax.ShapeDtypeStruct((8, STU), F32),
         ),
-        in_specs=[in_vmem] * 9,
+        in_specs=[in_vmem, in_vmem, in_hbm, in_vmem, in_hbm, in_vmem, in_vmem, in_vmem, in_hbm],
         out_specs=(pl.BlockSpec(memory_space=pltpu.SMEM), in_vmem, in_vmem),
         scratch_shapes=[
+            vm((FEAT, HID), BF16),
+            vm((HID, FEAT), BF16),
+            vm((STU, FEAT), BF16),
             vm((FEAT, HID), BF16),
             vm((HID, FEAT), BF16),
             vm((STU, FEAT), BF16),
@@ -494,9 +502,9 @@
             vm((CHUNKS, 4, HALF, HID), BF16),
             vm((CHUNKS, 3, HALF, HID), BF16),
             vm((CHUNKS, 4, HALF, HID), BF16),
-            vm((2, 3, 2, 4, HALF, FEAT), BF16),
-            vm((2, 3, 2, 4, HALF, FEAT), BF16),
-            vm((2, 2, 4, HALF, FEAT), F32),
+            vm((2, 4, 3, 2, HALF, FEAT), BF16),
+            vm((2, 4, 3, 2, HALF, FEAT), BF16),
+            vm((2, 4, 2, HALF, FEAT), F32),
             vm((2, 3, 2, HALF, FEAT), BF16),
             vm((2, 3, 2, HALF, FEAT), BF16),
             vm((2, HALF, FEAT), BF16),
@@ -531,6 +539,13 @@
         tokens, norm_gain, w_in, b_in, w_out, b_out,
         out_gain, student, w_exit,
     )
+    g_exit, g_student = pl.pallas_call(
+        place,
+        out_shape=(jax.ShapeDtypeStruct((32, FEAT), F32), jax.ShapeDtypeStruct((8, STU), F32)),
+        in_specs=[in_vmem] * 2,
+        out_specs=(in_vmem, in_vmem),
+        name="place",
+    )(g_exit, g_student)
     return loss.reshape(()), g_exit, g_student
 
 

time: 147 us -> 131 us (0.89)
  Pallas kernels: 142 us -> 129 us
  local copies, waits for them, and re-layouts: 2.91 us -> 0 us
    pallas_call x1, Pallas kernels: 142 us -> 127 us  [shards(): pl.pallas_call(kernel, out_shape=(jax.ShapeDtypeStruct((1, 1), F32), jax....]
    unnamed x2 -> x0, local copies, waits for them, and re-layouts: 2.91 us -> none
    pallas_call x0 -> x1, Pallas kernels: none -> 1.55 us  [shards(): pl.pallas_call(place, out_shape=(jax.ShapeDtypeStruct((32, FEAT), F32), j...]
where the time goes in v3:
time: 131 us
  Pallas kernels  129 us (98%)
  between operations  2.4 us (2%)
    pallas_call x1, Pallas kernels, shards(): pl.pallas_call(kernel, out_shape=(jax.ShapeDtypeStruct((1, 1), F32), jax....  127 us

profile of v3, /device:TPU:1, one launch (start us, length us, event | category | flops | bytes accessed | tf_op | source)
XLA Modules:
  0.0 131.2 jit_solution(14777938261067841779)
XLA Ops:
  0.6 127.3 %branch_and_exit.1 = (f32[1,1]{1,0:T(1,128)}, f32[32,768]{1,0:T(8,128)}, f32[8,1024]{1,0:T(8,128)}) custom-call(bf16[64,768]{1,0:T(8,128)(2,1)} %tokens.1, f32[768]{0:T(1024)} %norm_gain.1, bf16[768,768]{1,0:T(8,128)(2,1)} %w_in_hbm.1, f32[768]{0:T(1024)} %b_in.1, bf16[768,768]{1,0:T(8,128)(2,1)} %w_out_hbm.1, f32[768]{0:T(1024)} %b_out.1, f32[768]{0:T(1024)} %out_gain.1, ...), custom_call_target="tpu_custom_call" | custom-call | tf_op jit(solution)/shard_map/branch_and_exit/pallas_call | solution.py:476
  127.9 1.6 %place.1 = (f32[32,768]{1,0:T(8,128)}, f32[8,1024]{1,0:T(8,128)}) custom-call(f32[32,768]{1,0:T(8,128)} %get-tuple-element.9.a, f32[8,1024]{1,0:T(8,128)} %get-tuple-element.10.b), custom_call_target="tpu_custom_call" | custom-call | tf_op jit(solution)/shard_map/place/pallas_call | solution.py:542

commit v4 on v3

--- a/solution.py
+++ b/solution.py
@@ -23,7 +23,7 @@
 CHUNKS = 8
 LAG1, LAGF, LAG2, LAG3 = 1, 2, 3, 4
 BACK = 10
-ORDER = ((0, 0), (1, 0), (0, 1), (1, 1), (1, 3), (1, 2), (0, 3), (0, 2))
+ORDER = ((0, 0), (1, 0), (1, 1), (1, 3), (0, 1), (1, 2), (0, 3), (0, 2))
 
 
 def pick(n, table):
@@ -211,7 +211,7 @@
             a = a.reshape(4, HALF, TILE)
             part[k, :, :, cols] = a
             sent1[k, :, :, cols] = a.astype(BF16)
-        for i in range(1, 4):
+        for i in (3, 2, 1):
             rs_copy(k, i).start()
 
     def middle(k):

time: 131 us -> 129 us (0.985)
  Pallas kernels: 129 us -> 127 us
    pallas_call x1, Pallas kernels: 127 us -> 125 us  [shards(): pl.pallas_call(kernel, out_shape=(jax.ShapeDtypeStruct((1, 1), F32), jax....]
where the time goes in v4:
time: 129 us
  Pallas kernels  127 us (98%)
  between operations  2.4 us (2%)
    pallas_call x1, Pallas kernels, shards(): pl.pallas_call(kernel, out_shape=(jax.ShapeDtypeStruct((1, 1), F32), jax....  125 us

profile of v4, /device:TPU:1, one launch (start us, length us, event | category | flops | bytes accessed | tf_op | source)
XLA Modules:
  0.0 129.2 jit_solution(13892629363027341372)
XLA Ops:
  0.6 125.2 %branch_and_exit.1 = (f32[1,1]{1,0:T(1,128)}, f32[32,768]{1,0:T(8,128)}, f32[8,1024]{1,0:T(8,128)}) custom-call(bf16[64,768]{1,0:T(8,128)(2,1)} %tokens.1, f32[768]{0:T(1024)} %norm_gain.1, bf16[768,768]{1,0:T(8,128)(2,1)} %w_in_hbm.1, f32[768]{0:T(1024)} %b_in.1, bf16[768,768]{1,0:T(8,128)(2,1)} %w_out_hbm.1, f32[768]{0:T(1024)} %b_out.1, f32[768]{0:T(1024)} %out_gain.1, ...), custom_call_target="tpu_custom_call" | custom-call | tf_op jit(solution)/shard_map/branch_and_exit/pallas_call | solution.py:476
  125.9 1.6 %place.1 = (f32[32,768]{1,0:T(8,128)}, f32[8,1024]{1,0:T(8,128)}) custom-call(f32[32,768]{1,0:T(8,128)} %get-tuple-element.9.a, f32[8,1024]{1,0:T(8,128)} %get-tuple-element.10.b), custom_call_target="tpu_custom_call" | custom-call | tf_op jit(solution)/shard_map/place/pallas_call | solution.py:542

commit v5 on v4

--- a/solution.py
+++ b/solution.py
@@ -220,7 +220,7 @@
         pre = part[k, zl] + b_in[...].reshape(1, HID)
         pre += (got1[k, 0].astype(F32) + got1[k, 1].astype(F32)) + got1[k, 2].astype(F32)
         hidden[k, zl] = (0.5 * pre * (1.0 + lax.erf(pre * math.sqrt(0.5)))).astype(BF16)
-        for i in (2, 1):
+        for i in (1, 2):
             ag_copy(k, i).start()
 
     def forward(k):
@@ -327,7 +327,7 @@
         def _():
             reduce2(t - LAG3)
 
-        for when, what in ((2, gather_student), (3, predict), (5, transpose_student)):
+        for when, what in ((5, gather_student), (8, predict), (11, transpose_student)):
             pl.when(t == when)(what)
 
         @pl.when(t == BACK)

time: 129 us -> 130 us (level)
  no operation moved by 1% of the time
where the time goes in v5:
time: 130 us; the launch traced here: 129 us
  Pallas kernels  127 us (98%)
  between operations  2.4 us (2%)
    pallas_call x1, Pallas kernels, shards(): pl.pallas_call(kernel, out_shape=(jax.ShapeDtypeStruct((1, 1), F32), jax....  126 us

profile of v5, /device:TPU:1, one launch (start us, length us, event | category | flops | bytes accessed | tf_op | source)
XLA Modules:
  0.0 129.5 jit_solution(4131311917783681197)
XLA Ops:
  0.6 125.5 %branch_and_exit.1 = (f32[1,1]{1,0:T(1,128)}, f32[32,768]{1,0:T(8,128)}, f32[8,1024]{1,0:T(8,128)}) custom-call(bf16[64,768]{1,0:T(8,128)(2,1)} %tokens.1, f32[768]{0:T(1024)} %norm_gain.1, bf16[768,768]{1,0:T(8,128)(2,1)} %w_in_hbm.1, f32[768]{0:T(1024)} %b_in.1, bf16[768,768]{1,0:T(8,128)(2,1)} %w_out_hbm.1, f32[768]{0:T(1024)} %b_out.1, f32[768]{0:T(1024)} %out_gain.1, ...), custom_call_target="tpu_custom_call" | custom-call | tf_op jit(solution)/shard_map/branch_and_exit/pallas_call | solution.py:476
  126.2 1.6 %place.1 = (f32[32,768]{1,0:T(8,128)}, f32[8,1024]{1,0:T(8,128)}) custom-call(f32[32,768]{1,0:T(8,128)} %get-tuple-element.9.a, f32[8,1024]{1,0:T(8,128)} %get-tuple-element.10.b), custom_call_target="tpu_custom_call" | custom-call | tf_op jit(solution)/shard_map/place/pallas_call | solution.py:542
